TPU v7x, 32 devices: a whole 2x2x4 slice. The times are simulated.
32 devices in a mesh: dp: 8 (over z, x), seq: 4 (over y, core).
Axes of the slice: x: 2, y: 2, z: 4, core: 2. Of those that a mesh axis runs over, the one named last changes fastest.
Arguments:
- hidden: bfloat16 [8, 3072, 2560], P('dp', 'seq'), may hold values from -6 to 6
- log_decay: float32 [8, 40, 3072], P('dp', None, 'seq'), may hold values from -2 to 0, as said below
- input_weight: bfloat16 [2816, 2560], P(('dp', 'seq')), may hold values from -0.125 to 0.125
- conv_weight: bfloat16 [4, 2816], replicated, may hold values from -3 to 3
- conv_bias: float32 [2816], replicated, may hold values from -0.5 to 0.5
- skip_gain: float32 [40], replicated, may hold values from 0.5 to 1.5
Outputs:
- mixer_out: bfloat16 [8, 3072, 2560], P('dp', 'seq')
Inputs may be any that keep to these rules, and one draw needn't show every extreme that they name: `log_decay`: every value is negative.
All inputs are finite; a program needn't handle non-finite values.
Results may differ from a plain program's by a relative error of at most 0.0064.
Values may be sent and summed in bfloat16 or wider, within the bound.
A program may use at most 128 MiB of HBM per device.

v0:
```python
import jax
import jax.numpy as jnp
from jax import lax
from jax.sharding import PartitionSpec as P

HALF_HEADS = 40
HEAD_DIM = 64
STATE = 128
SPAN = 256
CONV = 4
INNER = 2560
COLS = 2816


def entering_2(part, axis, combine, identity):
    place = lax.axis_index(axis)
    gathered = jax.tree.map(lambda a: lax.all_gather(a, axis), part)
    state = jax.tree.map(lambda a, e: jnp.zeros_like(a) + jnp.asarray(e, a.dtype), part, identity)

    def one(lap, state):
        return combine(
            state, jax.tree.map(lambda a: lax.dynamic_index_in_dim(a, lap, 0, False), gathered)
        )

    return lax.fori_loop(0, place, one, state)


def passed_along(array, axis, by):
    peers = lax.axis_size(axis)
    pairs = [(i, i + by) for i in range(peers) if 0 <= i + by < peers]
    return lax.ppermute(array, axis, pairs)


def mixing_output(x_heads, b_span, c_span, cumulative, step_size):
    scores = jnp.dot(c_span, b_span.T, preferred_element_type=jnp.float32)
    span_len = cumulative.shape[1]
    causal = jnp.arange(span_len)[:, None] >= jnp.arange(span_len)[None, :]
    spread = jnp.where(causal[None], cumulative[:, :, None] - cumulative[:, None, :], -jnp.inf)
    mixing = (scores[None] * jnp.exp(spread) * step_size[:, None, :]).astype(jnp.bfloat16)
    return jnp.einsum("hqk,khp->qhp", mixing, x_heads, preferred_element_type=jnp.float32)


def span_state(x_heads, b_span, cumulative, step_size):
    weight = jnp.exp(cumulative[:, -1:] - cumulative) * step_size
    decayed = (x_heads * weight.T[:, :, None]).astype(jnp.bfloat16)
    return jnp.einsum("khp,kn->hpn", decayed, b_span, preferred_element_type=jnp.float32)


def state_output(c_span, entering, cumulative):
    readout = jnp.einsum(
        "qn,hpn->qhp", c_span.astype(jnp.float32), entering, precision=lax.Precision.HIGHEST
    )
    return jnp.exp(cumulative).T[:, :, None] * readout


def incoming(local_end, device_total):

    def combine(earlier, later_part):
        return (
            earlier[0] + later_part[0],
            jnp.exp(later_part[0])[:, None, None] * earlier[1] + later_part[1],
        )

    identity = (jnp.zeros_like(device_total), jnp.zeros_like(local_end))
    _, entering_dev = entering_2((device_total, local_end), "seq", combine, identity)
    return entering_dev


def body(hidden, log_decay, input_weight, conv_weight, conv_bias, skip_gain):
    token_rows = hidden[0]
    length = token_rows.shape[0]
    projected = lax.dot_general(
        token_rows,
        lax.all_gather(input_weight, ("dp", "seq"), axis=0, tiled=True),
        (((1,), (1,)), ((), ())),
        preferred_element_type=jnp.float32,
    ).astype(jnp.bfloat16)
    last_rows = projected[length - (CONV - 1) :]
    before_rows = passed_along(last_rows, "seq", 1)
    extended = jnp.concatenate([before_rows, projected], axis=0)
    filtered = jnp.broadcast_to(conv_bias[None, :], (length, COLS))
    for kernel_tap in range(CONV):
        filtered = (
            filtered
            + extended[kernel_tap : kernel_tap + length].astype(jnp.float32)
            * conv_weight[kernel_tap].astype(jnp.float32)[None, :]
        )
    active = jax.nn.silu(filtered).astype(jnp.bfloat16)
    span_count = length // SPAN
    x_all = active[:, :INNER].reshape(span_count, SPAN, HALF_HEADS, HEAD_DIM)
    b_all = active[:, INNER : INNER + STATE].reshape(span_count, SPAN, STATE)
    c_all = active[:, INNER + STATE :].reshape(span_count, SPAN, STATE)
    decay_spans = log_decay[0].reshape(HALF_HEADS, span_count, SPAN).transpose(1, 0, 2)
    cumulative = jnp.cumsum(decay_spans, axis=2)
    steps_all = -decay_spans
    totals = cumulative[:, :, -1]
    device_total = jnp.sum(totals, axis=0)
    zero_state = jnp.zeros((HALF_HEADS, HEAD_DIM, STATE), jnp.float32)

    def state_of(inputs):
        x_heads, b_span, cum_span, step_span = inputs
        return span_state(x_heads, b_span, cum_span, step_span)

    states = lax.map(state_of, (x_all, b_all, cumulative, steps_all))

    def gather_local(held_state, inputs):
        span_total, state_piece = inputs
        return (jnp.exp(span_total)[:, None, None] * held_state + state_piece, None)

    local_end, _ = lax.scan(gather_local, zero_state, (totals, states))
    entering_dev = incoming(local_end, device_total)

    def emit(held_state, inputs):
        x_heads, b_span, c_span, cum_span, step_span, span_total, state_piece = inputs
        outputs = mixing_output(x_heads, b_span, c_span, cum_span, step_span) + state_output(
            c_span, held_state, cum_span
        )
        return (jnp.exp(span_total)[:, None, None] * held_state + state_piece, outputs)

    _, outputs = lax.scan(
        emit, entering_dev, (x_all, b_all, c_all, cumulative, steps_all, totals, states)
    )
    outputs = outputs.reshape(length, HALF_HEADS, HEAD_DIM)
    final = outputs + skip_gain[None, :, None] * x_all.reshape(length, HALF_HEADS, HEAD_DIM).astype(
        jnp.float32
    )
    return final.reshape(1, length, INNER).astype(jnp.bfloat16)


def solution(mesh):
    placed = (P("dp", "seq", None), P("dp", None, "seq"), P(("dp", "seq"), None), P(), P(), P())
    return jax.shard_map(
        body, mesh=mesh, in_specs=placed, out_specs=P("dp", "seq", None), check_vma=False
    )
```

profile of v0, /device:TPU:5, one launch (start us, length us, event | category | flops | bytes accessed | tf_op | source)
XLA Modules:
  0.0 303.5 jit_solution(3257326404180995293)
XLA Ops:
  8.4 1.8 reduce-window.6
  11.6 104.7 %all-gather.5.cloned.1.call-done = bf16[2816,2560]{1,0:T(8,128)(2,1)} async-done(((bf16[88,2560]{1,0:T(8,128)(2,1)}), bf16[2816,2560]{1,0:T(8,128)(2,1)}) %all-gather.5.cloned.1.call-update) | async-done | bytes 14417936 | tf_op jit(solution)/shard_map/all_gather | solution.py:74
  116.3 16.5 %convolution_convert_fusion = bf16[768,2816]{1,0:T(8,128)(2,1)S(1)} fusion(bf16[2816,2560]{1,0:T(8,128)(2,1)} %all-gather.5.cloned.1.call-done, bf16[1,768,2560]{2,1,0:T(8,128)(2,1)} %param.14), kind=kOutput, calls=%fused_computation.56 | convolution fusion | flops 11075125248 | bytes 22675456 | tf_op jit(solution)/shard_map/dot_general | solution.py:72
  132.8 2.0 copy-done.2
  137.9 10.6 %multiply_convert_fusion.5 = bf16[768,2816]{1,0:T(8,128)(2,1)S(1)} fusion(bf16[768,2816]{1,0:T(8,128)(2,1)} %copy-done.2, bf16[3,2816]{1,0:T(4,128)(2,1)S(1)} %collective-permute-done, f32[2816]{0:T(1024)S(1)} %get-tuple-element.242, f32[2816]{0:T(1024)S(1)} %get-tuple-element.243, f32[2816]{0:T(1024)S(1)} %get-tuple-element.241, ...), kind=kLoop, calls=%fused_computation.52 | loop fusion | flops 56229888 | bytes 8723968 | tf_op jit(solution)/shard_map/convert_element_type | solution.py:88
  148.5 2.1 copy-done.1
  150.6 2.3 slice.68
  152.9 10.7 %reshape.90 = bf16[3,256,40,64]{3,2,1,0:T(8,128)(2,1)} reshape(bf16[768,2560]{1,0:T(8,128)(2,1)} %slice.68) | data formatting | bytes 7864320 | tf_op jit(solution)/shard_map/reshape | solution.py:90
  163.6 11.3 %copy.42 = bf16[3,256,40,64]{1,3,2,0:T(8,128)(2,1)} copy(bf16[3,256,40,64]{3,2,1,0:T(8,128)(2,1)} %reshape.90) | data formatting | bytes 7864320 | tf_op jit(solution)/shard_map/while | solution.py:104
  174.9 9.8 %while.45 = (s32[]{:T(128)}, f32[3,40,64,128]{3,2,1,0:T(8,128)}, bf16[3,256,40,64]{1,3,2,0:T(8,128)(2,1)}, f32[3,40,256]{2,1,0:T(8,128)S(1)}, f32[3,40,256]{2,0,...) while((s32[]{:T(128)}, f32[3,40,64,128]{3,2,1,0:T(8,128)}, bf16[3,256,40,64]{1,3,2,0:T(8,128)(2,1)}, ...), condition=%wide.region_4.5_spmd, body=%wide.region_3.4_spmd.sunk | while | flops 169758720 | bytes 3262517 | solution.py:104
  175.2 2.9 fusion.54
  178.5 2.9 fusion.54
  181.8 2.9 fusion.54
  184.7 4.7 %while.48 = (s32[]{:T(128)}, f32[40,64,128]{2,1,0:T(8,128)S(1)}, f32[3,40]{1,0:T(4,128)S(1)}, f32[3,40,64,128]{3,2,1,0:T(8,128)}, s32[]{:T(128)}, /*index=5*/s32[]{:T(128)}) while((s32[]{:T(128)}, f32[40,64,128]{2,1,0:T(8,128)S(1)}, f32[3,40]{1,0:T(4,128)S(1)}, f32[3,40,64,128]{3,2,1,0:T(8,128)}, s32[]{:T(128)}, ...), condition=%wide.region_6.7_spmd.clone, body=%wide.region_5.6_spmd.clone.sunk | while | flops 983043 | bytes 3932727 | solution.py:110
  192.1 7.3 %all-reduce = f32[160]{0:T(256)S(1)} all-reduce(f32[160]{0:T(256)S(1)} %dynamic-update-slice), channel_id=2, replica_groups=mesh['dp'=8,'seq'=4] {'seq'}, use_global_device_ids=true, to_apply=%add | all-reduce | flops 160 | bytes 1280
  199.6 30.6 %all-gather.7.cloned.1.call-done = f32[160,64,128]{2,1,0:T(8,128)} async-done(((f32[40,64,128]{2,1,0:T(8,128)}), f32[160,64,128]{2,1,0:T(8,128)}) %all-gather.7.cloned.1.call-update) | async-done | bytes 5242896 | tf_op jit(solution)/shard_map/all_gather | solution.py:17
  230.3 5.1 %while.46 = (s32[]{:T(128)}, f32[40,64,128]{2,1,0:T(8,128)S(1)}, s32[]{:T(128)}, f32[4,40]{1,0:T(4,128)S(1)}, f32[4,40,64,128]{3,2,1,0:T(8,128)}, /*index=5*/s32[]{:T(128)}, s32[]{:T(128)}, s32[]{:T(128)}) while((s32[]{:T(128)}, f32[40,64,128]{2,1,0:T(8,128)S(1)}, s32[]{:T(128)}, f32[4,40]{1,0:T(4,128)S(1)}, f32[4,40,64,128]{3,2,1,0:T(8,128)}, ...), condition=%wide.region_8.9_spmd, body=%wide.region_7.8_spmd.sunk | while | flops 655365 | bytes 3932767 | solution.py:25
  235.4 25.4 %while.47 = (s32[]{:T(128)}, f32[40,64,128]{2,1,0:T(8,128)S(1)}, f32[3,256,40,64]{1,3,2,0:T(8,128)}, f32[3,40]{1,0:T(4,128)S(1)}, f32[3,40,64,128]{3,2,1,0:T(8,1...) while((s32[]{:T(128)}, f32[40,64,128]{2,1,0:T(8,128)S(1)}, ...), condition=%wide.region_10.11_spmd, body=%wide.region_9.10_spmd.sunk | while | flops 1374093312 | bytes 15723105 | solution.py:120
  236.9 5.3 %bitcast_dynamic-update-slice_fusion.2 = f32[3,256,40,64]{1,3,2,0:T(8,128)} fusion(f32[3,256,40,64]{1,3,2,0:T(8,128)} %get-tuple-element.533, s32[]{:T(128)} %get-tuple-element.531, f32[256,40,64]{0,2,1:T(8,128)S(1)} %fusion.61, f32[40,256]{1,0:T(8,128)S(1)} %bitcast.132, f32[40,256]{1,0:T(8,128)S(1)} %get-tuple-element.451, ...), kind=kOutput, calls=%fused_computation.24.clone.1 | convolution fusion | flops 349962240 | bytes 7046144 | tf_op jit(solution)/shard_map/while/body/eval_jaxpr/hqk,khp->qhp/dot_general | solution.py:40
  245.4 5.3 %bitcast_dynamic-update-slice_fusion.2 = f32[3,256,40,64]{1,3,2,0:T(8,128)} fusion(f32[3,256,40,64]{1,3,2,0:T(8,128)} %get-tuple-element.533, s32[]{:T(128)} %get-tuple-element.531, f32[256,40,64]{0,2,1:T(8,128)S(1)} %fusion.61, f32[40,256]{1,0:T(8,128)S(1)} %bitcast.132, f32[40,256]{1,0:T(8,128)S(1)} %get-tuple-element.451, ...), kind=kOutput, calls=%fused_computation.24.clone.1 | convolution fusion | flops 349962240 | bytes 7046144 | tf_op jit(solution)/shard_map/while/body/eval_jaxpr/hqk,khp->qhp/dot_general | solution.py:40
  253.8 5.4 %bitcast_dynamic-update-slice_fusion.2 = f32[3,256,40,64]{1,3,2,0:T(8,128)} fusion(f32[3,256,40,64]{1,3,2,0:T(8,128)} %get-tuple-element.533, s32[]{:T(128)} %get-tuple-element.531, f32[256,40,64]{0,2,1:T(8,128)S(1)} %fusion.61, f32[40,256]{1,0:T(8,128)S(1)} %bitcast.132, f32[40,256]{1,0:T(8,128)S(1)} %get-tuple-element.451, ...), kind=kOutput, calls=%fused_computation.24.clone.1 | convolution fusion | flops 349962240 | bytes 7046144 | tf_op jit(solution)/shard_map/while/body/eval_jaxpr/hqk,khp->qhp/dot_general | solution.py:40
  260.8 14.6 %copy.51 = f32[3,256,40,64]{3,2,1,0:T(8,128)} copy(f32[3,256,40,64]{1,3,2,0:T(8,128)} %get-tuple-element.158) | data formatting | bytes 15728640 | tf_op jit(solution)/shard_map/reshape | solution.py:123
  275.4 13.7 %reshape.89 = f32[768,2560]{1,0:T(8,128)} reshape(f32[3,256,40,64]{3,2,1,0:T(8,128)} %copy.51) | data formatting | bytes 15728640 | tf_op jit(solution)/shard_map/reshape | solution.py:123
  289.1 7.5 %fusion.34 = bf16[1,768,2560]{2,1,0:T(8,128)(2,1)} fusion(f32[768,2560]{1,0:T(8,128)} %reshape.89, f32[2560]{0:T(1024)S(1)} %mul.153, bf16[768,2816]{1,0:T(8,128)(2,1)} %copy-done.1), kind=kLoop, calls=%fused_computation.60 | loop fusion | flops 7864320 | bytes 15738880 | tf_op jit(solution)/shard_map/convert_element_type | solution.py:127
  (95 shorter events, 28.3 us)
Async XLA Ops:
  6.5 109.8 %all-gather.5.cloned.1.call-start = ((), (), s32[]{:S(2)}) async-start(), calls=%async_computation | async-start | bytes 14868480 | tf_op jit(solution)/shard_map/all_gather | solution.py:74
  7.3 222.9 %all-gather.7.cloned.1.call-start = ((), (), s32[]{:S(2)}) async-start(), calls=%async_computation.1 | async-start | bytes 6553600 | tf_op jit(solution)/shard_map/all_gather | solution.py:17
  11.6 126.3 %copy-start.3 = (f32[2816]{0:T(1024)S(1)}, f32[2816]{0:T(1024)}, u32[]{:S(2)}) copy-start(f32[2816]{0:T(1024)} %param.18) | copy-start | bytes 33796
  132.8 2.0 copy-start.2
  134.8 3.1 %collective-permute-start = (bf16[3,2816]{1,0:T(4,128)(2,1)S(1)}, bf16[3,2816]{1,0:T(4,128)(2,1)S(1)}, u32[]{:S(2)}, u32[]{:S(2)}) collective-permute-start(bf16[3,2816]{1,0:T(4,128)(2,1)S(1)} %slice.63), channel_id=1, source_target_pairs={{0,1},{1,2},{2,3},{4,5},{5,6},{6,7},{8,9},{9,10},{10,11},{12,13},{... | collective-permute-start | bytes 50696 | tf_op jit(solution)/shard_map/ppermute | solution.py:31
  148.5 2.1 copy-start.1
  184.7 5.9 %copy-start.5 = (u32[32]{0:T(128)S(1)}, u32[32]{0:T(128)}, u32[]{:S(2)}) copy-start(u32[32]{0:T(128)} %constant.77) | copy-start | bytes 388
  184.7 14.7 %copy-start.4 = (f32[40]{0:T(128)S(1)}, f32[40]{0:T(128)}, u32[]{:S(2)}) copy-start(f32[40]{0:T(128)} %param.19) | copy-start | bytes 484
  189.4 1.1 copy-start
Sparse Core Ops, SparseCore 0:
  10.2 106.0 all-gather.4
  190.6 39.4 all-gather.6
where the time goes:
time: 305 us; the launch traced here: 303 us
  waiting for transfers between devices  138 us (45%)
  local copies, waits for them, and re-layouts  61.6 us (20%)
  matrix products  45.3 us (15%)
  other arithmetic  35.5 us (12%)
  between operations  14.2 us (5%)
  blocking collectives  7.28 us (2%)
    all_gather x1, waiting for transfers between devices, body(): lax.all_gather(input_weight, ('dp', 'seq'), axis=0, tiled=True)  105 us
    all_gather x1, waiting for transfers between devices, entering_2(): gathered = jax.tree.map(lambda a: lax.all_gather(a, axis), part)  30.6 us
    reshape x2, local copies, waits for them, and re-layouts, body(): outputs = outputs.reshape(length, HALF_HEADS, HEAD_DIM)  28.3 us
    dot_general x1, matrix products, body(): lax.dot_general(token_rows, lax.all_gather(input_weight, ('dp', 'seq'), a...  16.5 us
    dot_general x3, matrix products, mixing_output(): jnp.einsum('hqk,khp->qhp', mixing, x_heads, preferred_element_type=jnp.fl...  16 us
    while x1, local copies, waits for them, and re-layouts, body(): states = lax.map(state_of, (x_all, b_all, cumulative, steps_all))  11.3 us
    reshape x1, local copies, waits for them, and re-layouts, body(): x_all = active[:, :INNER].reshape(span_count, SPAN, HALF_HEADS, HEAD_DIM)  10.7 us
    convert_element_type x1, other arithmetic, body(): active = jax.nn.silu(filtered).astype(jnp.bfloat16)  10.6 us
  transfers between devices with their start and end apart: 3, of which 3 were waited for; matrix products, arithmetic and copies ran while one was open for 2% of the time, Pallas kernels for 0%

commit v1 on v0

v1 whole, which is shorter than its diff:
```python
import functools

import jax
import jax.numpy as jnp
from jax import lax
from jax.experimental import pallas as pl
from jax.experimental.pallas import tpu as pltpu
from jax.sharding import PartitionSpec as P

HEADS = 40
HEAD_DIM = 64
STATE = 128
SPAN = 256
CONV = 4
INNER = 2560
COLS = 2816
GROUP = 8
GROUPS = HEADS // GROUP
CHUNK = 256
HALO = 16
TILE = 64
LOG2E = 1.4426950408889634
F32 = jnp.float32
BF16 = jnp.bfloat16
NT = (((1,), (1,)), ((), ()))


def split_parts(both):
    high = both.astype(BF16).astype(F32)
    lane = lax.broadcasted_iota(jnp.int32, both.shape, 1)
    return jnp.where(lane < HEADS, high, both - high).astype(BF16)


def mixer_kernel(
    spans, peers,
    proj, taps, bias, weight, growth, spread, decay, skip, column, row,
    out,
    halo, previous, act, bt, states, local, total, scores, sending, entering,
    halo_sems, state_sems,
):
    place = lax.axis_index("seq")
    length = spans * SPAN
    after, before = lax.rem(place + 1, peers), lax.rem(place + peers - 1, peers)
    barrier = pltpu.get_barrier_semaphore()
    for neighbour in (before, after):
        pl.semaphore_signal(
            barrier, inc=1, device_id={"seq": neighbour}, device_id_type=pl.DeviceIdType.MESH
        )
    pl.semaphore_wait(barrier, 2)
    has_after = place < peers - 1
    has_before = place > 0

    halo_copy = pltpu.make_async_remote_copy(
        src_ref=proj.at[pl.ds(length - HALO, HALO)], dst_ref=halo,
        send_sem=halo_sems.at[0], recv_sem=halo_sems.at[1],
        device_id={"seq": after}, device_id_type=pl.DeviceIdType.MESH,
    )
    state_copy = pltpu.make_async_remote_copy(
        src_ref=sending, dst_ref=entering,
        send_sem=state_sems.at[0], recv_sem=state_sems.at[1],
        device_id={"seq": after}, device_id_type=pl.DeviceIdType.MESH,
    )

    @pl.when(has_after)
    def _():
        halo_copy.start()

    def rows_of(span):
        return pl.ds(pl.multiple_of(span * SPAN, SPAN), SPAN)

    def lanes_of(chunk, width=CHUNK):
        return pl.ds(pl.multiple_of(chunk * width, width), width)

    @pl.loop(0, spans)
    def _(lap):
        span = spans - 1 - lap
        rows = rows_of(span)

        @pl.when(span > 0)
        def _():
            start = pl.multiple_of(jnp.maximum(span * SPAN - HALO, 0), HALO)
            previous[...] = proj[pl.ds(start, HALO), :]

        @pl.when(span == 0)
        def _():
            @pl.when(has_before)
            def _():
                halo_copy.wait_recv()
                previous[...] = halo[...]

            @pl.when(jnp.logical_not(has_before))
            def _():
                previous[...] = jnp.zeros_like(previous)

        @pl.loop(0, COLS // CHUNK)
        def _(chunk):
            lanes = lanes_of(chunk)
            tap = [taps[k : k + 1, lanes] for k in range(CONV)]
            offset = bias[:, lanes]
            for part in range(SPAN // TILE):
                start = pl.multiple_of(span * SPAN + part * TILE, TILE)
                here = proj[pl.ds(start, TILE), lanes].astype(F32)
                if part == 0:
                    ahead = previous[:, lanes].astype(F32)
                else:
                    earlier = pl.multiple_of(start - HALO, HALO)
                    ahead = proj[pl.ds(earlier, HALO), lanes].astype(F32)
                both = jnp.concatenate([ahead[HALO - 8 :], here], axis=0)
                value = offset + here * tap[CONV - 1]
                for k in range(CONV - 1):
                    at = 8 - (CONV - 1) + k
                    value = value + both[at : at + TILE] * tap[k]
                act[pl.ds(start, TILE), lanes] = (value / (1.0 + jnp.exp(-value))).astype(BF16)

        bt[...] = act[rows, INNER : INNER + STATE].astype(F32).T.astype(BF16)
        parts = split_parts(weight[rows, :])

        @pl.loop(0, INNER // CHUNK)
        def _(chunk):
            lanes = lanes_of(chunk)
            scale = jnp.dot(parts, spread[:, lanes], preferred_element_type=F32)
            decayed = (act[rows, lanes].astype(F32) * scale).astype(BF16)
            states[span, :, lanes] = jnp.dot(bt[...], decayed, preferred_element_type=F32)

    @pl.loop(0, INNER // CHUNK)
    def _(chunk):
        lanes = lanes_of(chunk)
        held = states[0, :, lanes]
        for span in range(1, spans):
            held = decay[span : span + 1, lanes] * held + states[span, :, lanes]
        local[:, lanes] = held

    def relay():
        @pl.when(has_before)
        def _():
            state_copy.wait_recv()

        @pl.when(jnp.logical_not(has_before))
        def _():
            entering[...] = jnp.zeros_like(entering)

        @pl.when(has_after)
        def _():
            @pl.loop(0, INNER // CHUNK)
            def _(chunk):
                lanes = lanes_of(chunk)
                whole = decay[spans : spans + 1, lanes]
                sending[:, lanes] = (
                    whole * entering[:, lanes].astype(F32) + local[:, lanes]
                ).astype(BF16)

            state_copy.start()

    @pl.when(place <= 1)
    def _():
        relay()

    @pl.loop(0, spans)
    def _(span):
        rows = rows_of(span)
        product = lax.dot_general(
            act[rows, INNER + STATE :], act[rows, INNER : INNER + STATE], NT,
            preferred_element_type=F32,
        )
        later = lax.broadcasted_iota(jnp.int32, (SPAN, SPAN), 0)
        sooner = lax.broadcasted_iota(jnp.int32, (SPAN, SPAN), 1)
        scores[...] = jnp.where(later >= sooner, product, 0.0)
        half = SPAN // 2
        first = lax.broadcasted_iota(jnp.int32, (SPAN, 2 * HEAD_DIM), 1) < HEAD_DIM

        @pl.loop(0, GROUPS)
        def _(group):
            for pair in range(GROUP // 2):
                lanes = pl.ds(
                    pl.multiple_of(group * (GROUP * HEAD_DIM) + pair * 128, 128), 128
                )
                heads_in = act[rows, lanes]
                given = []
                for head in (2 * pair, 2 * pair + 1):
                    at_later = column[group, rows, head : head + 1]
                    at_sooner = row[group, head : head + 1, rows]
                    upper = scores[:half, :half] * jnp.exp2(
                        jnp.minimum(at_later[:half] - at_sooner[:, :half], 100.0)
                    )
                    lower = scores[half:, :] * jnp.exp2(
                        jnp.minimum(at_later[half:] - at_sooner, 100.0)
                    )
                    given.append(
                        jnp.concatenate(
                            [
                                jnp.dot(
                                    upper.astype(BF16), heads_in[:half],
                                    preferred_element_type=F32,
                                ),
                                jnp.dot(
                                    lower.astype(BF16), heads_in, preferred_element_type=F32
                                ),
                            ],
                            axis=0,
                        )
                    )
                total[rows, lanes] = (
                    jnp.where(first, given[0], given[1])
                    + skip[:, lanes] * heads_in.astype(F32)
                )

    @pl.when(place > 1)
    def _():
        relay()

    @pl.loop(0, INNER // CHUNK)
    def _(chunk):
        lanes = lanes_of(chunk)
        held = entering[:, lanes].astype(F32)
        for span in range(spans):
            rows = pl.ds(span * SPAN, SPAN)
            grown = jnp.dot(
                split_parts(growth[rows, :]), spread[:, lanes], preferred_element_type=F32
            )
            read = jnp.dot(
                act[rows, INNER + STATE :], held.astype(BF16), preferred_element_type=F32
            )
            out[rows, lanes] = (total[rows, lanes] + grown * read).astype(BF16)
            if span < spans - 1:
                held = decay[span : span + 1, lanes] * held + states[span, :, lanes]

    @pl.when(has_after)
    def _():
        halo_copy.wait_send()
        state_copy.wait_send()


def mixer(projected, log_decay, conv_weight, conv_bias, skip_gain):
    length = projected.shape[0]
    spans = length // SPAN
    peers = lax.axis_size("seq")
    step = -log_decay
    cum = jnp.cumsum(log_decay.reshape(HEADS, spans, SPAN), axis=2)
    last = cum[:, :, -1:]
    weight = jnp.exp(last - cum).reshape(HEADS, length) * step
    flat = cum.reshape(HEADS, length)

    def doubled(a):
        return jnp.pad(jnp.concatenate([a, a], axis=0).T, ((0, 0), (0, 128 - 2 * HEADS)))

    grouped = (flat * LOG2E).reshape(GROUPS, GROUP, length)
    column = grouped.transpose(0, 2, 1)
    row = grouped - jnp.log2(step).reshape(GROUPS, GROUP, length)
    totals = last[:, :, 0].T
    totals = jnp.concatenate([totals, jnp.sum(totals, axis=0, keepdims=True)], axis=0)
    decay = jnp.repeat(jnp.exp(totals), HEAD_DIM, axis=1)
    decay = jnp.pad(decay, ((0, -decay.shape[0] % 8), (0, 0)))
    head_of = jnp.arange(INNER)[None, :] // HEAD_DIM
    part = jnp.arange(128)[:, None]
    spread = ((part % HEADS == head_of) & (part < 2 * HEADS)).astype(BF16)
    taps = jnp.pad(conv_weight.astype(F32), ((0, 8 - CONV), (0, 0)))
    vmem = pl.BlockSpec(memory_space=pltpu.VMEM)
    return pl.pallas_call(
        functools.partial(mixer_kernel, spans, peers),
        out_shape=jax.ShapeDtypeStruct((length, INNER), BF16),
        in_specs=[vmem] * 10,
        out_specs=vmem,
        scratch_shapes=[
            pltpu.VMEM((HALO, COLS), BF16),
            pltpu.VMEM((HALO, COLS), BF16),
            pltpu.VMEM((length, COLS), BF16),
            pltpu.VMEM((STATE, SPAN), BF16),
            pltpu.VMEM((spans, STATE, INNER), F32),
            pltpu.VMEM((STATE, INNER), F32),
            pltpu.VMEM((length, INNER), F32),
            pltpu.VMEM((SPAN, SPAN), F32),
            pltpu.VMEM((STATE, INNER), BF16),
            pltpu.VMEM((STATE, INNER), BF16),
            pltpu.SemaphoreType.DMA((2,)),
            pltpu.SemaphoreType.DMA((2,)),
        ],
        compiler_params=pltpu.CompilerParams(
            collective_id=0, has_side_effects=True, vmem_limit_bytes=56 * 2**20
        ),
        cost_estimate=pl.CostEstimate(
            flops=8 * 10**9, bytes_accessed=16 * 10**6, transcendentals=12 * 10**6
        ),
        name="mixer",
    )(
        projected, taps, conv_bias[None, :], doubled(weight), doubled(jnp.exp(flat)),
        spread, decay, jnp.repeat(skip_gain, HEAD_DIM)[None, :], column, row,
    )


def body(hidden, log_decay, input_weight, conv_weight, conv_bias, skip_gain):
    projected = lax.dot_general(
        hidden[0],
        lax.all_gather(input_weight, ("dp", "seq"), axis=0, tiled=True),
        NT,
        preferred_element_type=F32,
    ).astype(BF16)
    return mixer(projected, log_decay[0], conv_weight, conv_bias, skip_gain)[None]


def solution(mesh):
    placed = (P("dp", "seq", None), P("dp", None, "seq"), P(("dp", "seq"), None), P(), P(), P())
    return jax.shard_map(
        body, mesh=mesh, in_specs=placed, out_specs=P("dp", "seq", None), check_vma=False
    )
```

time: 305 us -> 187 us (0.61)
  local copies, waits for them, and re-layouts: 61.6 us -> 12.9 us
  waiting for transfers between devices: 138 us -> 95.1 us
  Pallas kernels: 0 us -> 41.6 us
  other arithmetic: 35.5 us -> 5.86 us
  matrix products: 45.3 us -> 18.1 us
  blocking collectives: 7.28 us -> 0 us
    pallas_call x0 -> x1, Pallas kernels: none -> 41.6 us  [mixer(): pl.pallas_call(functools.partial(mixer_kernel, spans, peers), out_shape=j...]
    reshape x5 -> x3, local copies, waits for them, and re-layouts: 39.2 us -> 1.07 us  [the longest x2 28.3 us: body(): outputs = outputs.reshape(length, HALF_HEADS, HEAD_DIM)]
    all_gather x1 -> x0, waiting for transfers between devices: 30.6 us -> none  [entering_2(): gathered = jax.tree.map(lambda a: lax.all_gather(a, axis), part)]
    dot_general x13 -> x1, matrix products: 45.3 us -> 18.1 us  [body(): lax.dot_general(hidden[0], lax.all_gather(input_weight, ('dp', 'seq'), ax...]
    convert_element_type x2 -> x1, other arithmetic: 18.1 us -> 1.1 us  [mixer(): spread = ((part % HEADS == head_of) & (part < 2 * HEADS)).astype(BF16)]
    add x9 -> x0, other arithmetic: 14.1 us -> none  [the longest x3 4.73 us: combine(): jnp.exp(later_part[0])[:, None, None] * earlier[1] + later_part[1]]
    while x1 -> x0, local copies, waits for them, and re-layouts: 11.3 us -> none  [body(): states = lax.map(state_of, (x_all, b_all, cumulative, steps_all))]
    all_gather x1, waiting for transfers between devices: 105 us -> 94.4 us  [body(): lax.all_gather(input_weight, ('dp', 'seq'), axis=0, tiled=True)]
  transfers between devices with their start and end apart: 3 -> 1, of which waited for: 3 -> 1; matrix products, arithmetic and copies ran while one was open for 2% -> 8% of each run, Pallas kernels for 0% -> 0%
where the time goes in v1:
time: 187 us
  waiting for transfers between devices  95.1 us (51%)
  Pallas kernels  41.6 us (22%)
  matrix products  18.1 us (10%)
  between operations  13.5 us (7%)
  local copies, waits for them, and re-layouts  12.9 us (7%)
  other arithmetic  5.86 us (3%)
    all_gather x1, waiting for transfers between devices, body(): lax.all_gather(input_weight, ('dp', 'seq'), axis=0, tiled=True)  94.4 us
    pallas_call x1, Pallas kernels, mixer(): pl.pallas_call(functools.partial(mixer_kernel, spans, peers), out_shape=j...  41.6 us
    dot_general x1, matrix products, body(): lax.dot_general(hidden[0], lax.all_gather(input_weight, ('dp', 'seq'), ax...  18.1 us
    unnamed x5, local copies, waits for them, and re-layouts  4.3 us
  transfers between devices with their start and end apart: 1, of which 1 were waited for; matrix products, arithmetic and copies ran while one was open for 8% of the time, Pallas kernels for 0%

profile of v1, /device:TPU:5, one launch (start us, length us, event | category | flops | bytes accessed | tf_op | source)
XLA Modules:
  0.0 187.1 jit_solution(18363683462052336802)
XLA Ops:
  6.5 0.7 all-gather.2.cloned.1.call-update
  7.3 0.9 neg.8
  8.2 1.0 reshape.93
  9.1 1.3 broadcast_in_dim.17.bias
  10.5 0.7 broadcast_in_dim.20
  11.2 0.7 broadcast_in_dim_reshape.3.skip
  11.9 1.8 reduce-window.6
  13.9 0.1 broadcast_multiply_fusion
  14.2 0.2 copy.35
  14.4 0.2 slice_reduce_fusion
  14.8 0.7 pad.21.decay
  15.5 0.2 copy.36
  15.6 0.1 bitcast_exponential_fusion
  15.8 0.3 maximum_bitcast_fusion
  16.0 0.8 pad.19.weight
  16.8 0.8 pad.20.growth
  17.6 1.8 copy.38.column
  19.5 0.7 bitcast_subtract_fusion.1.row
  20.2 0.6 pad_convert_fusion.taps
  20.8 1.1 and_convert_fusion.spread
  21.9 94.4 %all-gather.2.cloned.1.call-done = bf16[2816,2560]{1,0:T(8,128)(2,1)} async-done(((bf16[88,2560]{1,0:T(8,128)(2,1)}), bf16[2816,2560]{1,0:T(8,128)(2,1)}) %all-gather.2.cloned.1.call-update) | async-done | bytes 14417936 | tf_op jit(solution)/shard_map/all_gather | solution.py:293
  116.3 18.1 %convolution_convert_fusion.proj = bf16[768,2816]{1,0:T(8,128)(2,1)} fusion(bf16[2816,2560]{1,0:T(8,128)(2,1)} %all-gather.2.cloned.1.call-done, bf16[1,768,2560]{2,1,0:T(8,128)(2,1)} %param.6), kind=kOutput, calls=%fused_computation | convolution fusion | flops 11075125248 | bytes 22675456 | tf_op jit(solution)/shard_map/dot_general | solution.py:291
  134.4 41.6 %mixer.1 = bf16[768,2560]{1,0:T(8,128)(2,1)} custom-call(bf16[768,2816]{1,0:T(8,128)(2,1)} %convolution_convert_fusion.proj, f32[8,2816]{1,0:T(8,128)} %pad_convert_fusion.taps, f32[1,2816]{1,0:T(1,128)} %broadcast_in_dim.17.bias, f32[768,128]{1,0:T(8,128)} %pad.19.weight, f32[768,128]{1,0:T(8,128)} %pad.20.growth, ...), custom_call_target="tpu_custom_call" | custom-call | flops 8000000000 | bytes 16000000 | tf_op jit(solution)/shard_map/mixer/pallas_call | solution.py:258
  176.0 4.3 %copy.42 = bf16[1,768,2560]{2,1,0:T(8,128)(2,1)} copy(bf16[1,768,2560]{2,1,0:T(8,128)(2,1)} %bitcast.31) | data formatting | bytes 7864320
  (20 shorter events, 0.6 us)
Async XLA Ops:
  6.5 109.8 %all-gather.2.cloned.1.call-start = ((), (), s32[]{:S(2)}) async-start(), calls=%async_computation | async-start | bytes 14868480 | tf_op jit(solution)/shard_map/all_gather | solution.py:293
  14.4 5.1 %copy-start = (f32[1,40,768]{2,1,0:T(8,128)S(1)}, f32[1,40,768]{2,1,0:T(8,128)}, u32[]{:S(2)}) copy-start(f32[1,40,768]{2,1,0:T(8,128)} %param.7) | copy-start | bytes 368644
  14.8 5.4 %copy-start.1 = (bf16[4,2816]{1,0:T(4,128)(2,1)S(1)}, bf16[4,2816]{1,0:T(4,128)(2,1)}, u32[]{:S(2)}) copy-start(bf16[4,2816]{1,0:T(4,128)(2,1)} %param.9) | copy-start | bytes 67588
Sparse Core Ops, SparseCore 0:
  10.2 106.0 all-gather.1

commit v2 on v1

--- a/solution.py
+++ b/solution.py
@@ -287,10 +287,210 @@
     )
 
 
+ORDER = (0, -1, 1, -2, 2, -3, 3)
+BY_Z, BY_X, BY_Y, BY_X_HALF, BY_Y_HALF, FROM_OWN, FROM_X, FROM_Y, FROM_XY = range(9)
+
+
+def gather_kernel(layers, shard, whole, send_sems, up_sems, recv_sems, own_sem):
+    dp, seq = lax.axis_index("dp"), lax.axis_index("seq")
+    z, x = dp // 2, lax.rem(dp, 2)
+    y, core = seq // 2, lax.rem(seq, 2)
+    x_peer = (z * 2 + 1 - x, seq)
+    y_peer = (dp, (1 - y) * 2 + core)
+    core_peer = (dp, y * 2 + 1 - core)
+    above, below = (dp + 2, seq), (dp - 2, seq)
+    has_above, has_below = z < layers - 1, z > 0
+
+    barrier = pltpu.get_barrier_semaphore()
+
+    def greet(peer):
+        pl.semaphore_signal(
+            barrier, inc=1, device_id=peer, device_id_type=pl.DeviceIdType.MESH
+        )
+
+    for peer in (x_peer, y_peer, core_peer):
+        greet(peer)
+
+    @pl.when(has_above)
+    def _():
+        greet(above)
+
+    @pl.when(has_below)
+    def _():
+        greet(below)
+
+    peers = 3 + has_above.astype(jnp.int32) + has_below.astype(jnp.int32)
+    pl.semaphore_wait(barrier, peers)
+
+    half = whole.shape[2] // 2
+    low, high = pl.ds(0, half), pl.ds(half, half)
+
+    def slot(away, other_x=False, other_y=False):
+        at_x = 1 - x if other_x else x
+        at_y = 1 - y if other_y else y
+        return (((z + away) * 2 + at_x) * 2 + at_y) * 2 + core
+
+    def copy(src, dst, send, recv, peer):
+        return pltpu.make_async_remote_copy(
+            src_ref=src, dst_ref=dst, send_sem=send, recv_sem=recv,
+            device_id=peer, device_id_type=pl.DeviceIdType.MESH,
+        )
+
+    def moved(place, kind, other_x, other_y, peer, lanes=None):
+        at = slot(ORDER[place], other_x, other_y)
+        dst = whole.at[at] if lanes is None else whole.at[at, :, lanes]
+        src = shard if place == 0 and not other_x and not other_y else dst
+        return copy(src, dst, send_sems.at[place, kind], recv_sems.at[place, kind], peer)
+
+    def by_x(place):
+        return moved(place, BY_X, False, False, x_peer)
+
+    def by_y(place):
+        return moved(place, BY_Y, False, False, y_peer)
+
+    def by_x_half(place):
+        return moved(place, BY_X_HALF, False, True, x_peer, high)
+
+    def by_y_half(place):
+        return moved(place, BY_Y_HALF, True, False, y_peer, low)
+
+    def to_core(place, kind):
+        return moved(
+            place, kind, kind in (FROM_X, FROM_XY), kind in (FROM_Y, FROM_XY), core_peer
+        )
+
+    def relayed(place, up):
+        away = ORDER[place]
+        then = ORDER.index(away - 1 if up else away + 1)
+        at = slot(away)
+        return copy(
+            shard if place == 0 else whole.at[at], whole.at[at],
+            up_sems.at[place] if up else send_sems.at[place, BY_Z],
+            recv_sems.at[then, BY_Z], above if up else below,
+        )
+
+    def arrived(place, kind, other_x, other_y, lanes=None):
+        at = slot(ORDER[place], other_x, other_y)
+        dst = whole.at[at] if lanes is None else whole.at[at, :, lanes]
+        copy(dst, dst, own_sem, recv_sems.at[place, kind], core_peer).wait_recv()
+
+    def exists(place):
+        away = ORDER[place]
+        return jnp.logical_and(z + away >= 0, z + away < layers)
+
+    def relays(place):
+        away = ORDER[place]
+        found = []
+        if -layers + 1 < away <= 0:
+            found.append((jnp.logical_and(has_above, z + away >= 0), True))
+        if layers - 1 > away >= 0:
+            found.append((jnp.logical_and(has_below, z + away < layers), False))
+        return found
+
+    def column_step(place):
+        for there, up in relays(place):
+            @pl.when(there)
+            def _(up=up):
+                if place and up == relays(place)[0][1]:
+                    arrived(place, BY_Z, False, False)
+                relayed(place, up).start()
+
+        ends = not relays(place)
+
+        @pl.when(exists(place))
+        def _():
+            if place:
+                if ends:
+                    arrived(place, BY_Z, False, False)
+                else:
+                    @pl.when(jnp.logical_not(relays(place)[0][0]))
+                    def _():
+                        arrived(place, BY_Z, False, False)
+            by_x(place).start()
+            by_y(place).start()
+            to_core(place, FROM_OWN).start()
+
+    def plane_step(place):
+        @pl.when(exists(place))
+        def _():
+            arrived(place, BY_X, True, False)
+            by_y_half(place).start()
+            to_core(place, FROM_X).start()
+            arrived(place, BY_Y, False, True)
+            by_x_half(place).start()
+            to_core(place, FROM_Y).start()
+
+    def corner_step(place):
+        @pl.when(exists(place))
+        def _():
+            arrived(place, BY_X_HALF, True, True, high)
+            arrived(place, BY_Y_HALF, True, True, low)
+            to_core(place, FROM_XY).start()
+
+    own = pltpu.make_async_copy(shard, whole.at[slot(0)], own_sem)
+    places = range(2 * layers - 1)
+    for place in places:
+        column_step(place)
+        if place == 0:
+            own.start()
+        if place >= 2:
+            plane_step(place - 2)
+        if place >= 4:
+            corner_step(place - 4)
+    for place in places[-2:]:
+        plane_step(place)
+    for place in places[-4:]:
+        corner_step(place)
+    own.wait()
+    for place in places:
+        for there, up in relays(place):
+            @pl.when(there)
+            def _(up=up):
+                relayed(place, up).wait_send()
+
+        @pl.when(exists(place))
+        def _():
+            for sent in (
+                by_x(place), by_y(place), by_x_half(place), by_y_half(place),
+                to_core(place, FROM_OWN), to_core(place, FROM_X),
+                to_core(place, FROM_Y), to_core(place, FROM_XY),
+            ):
+                sent.wait_send()
+            for kind in (FROM_OWN, FROM_X, FROM_Y, FROM_XY):
+                at = slot(
+                    ORDER[place], kind in (FROM_X, FROM_XY), kind in (FROM_Y, FROM_XY)
+                ) + 1 - 2 * core
+                dst = whole.at[at]
+                copy(dst, dst, own_sem, recv_sems.at[place, kind], core_peer).wait_recv()
+
+
+def gathered(input_weight):
+    devices = lax.axis_size("dp"), lax.axis_size("seq")
+    if devices != (8, 4):
+        return lax.all_gather(input_weight, ("dp", "seq"), axis=0, tiled=True)
+    rows, depth = input_weight.shape
+    anywhere = pl.BlockSpec(memory_space=pl.ANY)
+    whole = pl.pallas_call(
+        functools.partial(gather_kernel, devices[0] // 2),
+        out_shape=jax.ShapeDtypeStruct((devices[0] * devices[1], rows, depth), BF16),
+        in_specs=[anywhere],
+        out_specs=anywhere,
+        scratch_shapes=[
+            pltpu.SemaphoreType.DMA((7, 9)),
+            pltpu.SemaphoreType.DMA((7,)),
+            pltpu.SemaphoreType.DMA((7, 9)),
+            pltpu.SemaphoreType.DMA,
+        ],
+        compiler_params=pltpu.CompilerParams(collective_id=1, has_side_effects=True),
+        name="gather",
+    )(input_weight)
+    return whole.reshape(devices[0] * devices[1] * rows, depth)
+
+
 def body(hidden, log_decay, input_weight, conv_weight, conv_bias, skip_gain):
     projected = lax.dot_general(
         hidden[0],
-        lax.all_gather(input_weight, ("dp", "seq"), axis=0, tiled=True),
+        gathered(input_weight),
         NT,
         preferred_element_type=F32,
     ).astype(BF16)

time: 187 us -> 143 us (0.76)
  waiting for transfers between devices: 95.1 us -> 0 us
  Pallas kernels: 41.6 us -> 109 us
  between operations: 13.5 us -> 0.17 us
  local copies, waits for them, and re-layouts: 12.9 us -> 10.7 us
    all_gather x1 -> x0, waiting for transfers between devices: 94.4 us -> none  [body(): lax.all_gather(input_weight, ('dp', 'seq'), axis=0, tiled=True)]
    pallas_call x0 -> x1, Pallas kernels: none -> 67 us  [gathered(): pl.pallas_call(functools.partial(gather_kernel, devices[0] // 2), out_sha...]
    unnamed x5 -> x9, local copies, waits for them, and re-layouts: 4.3 us -> 4.31 us
  transfers between devices with their start and end apart: 1 -> 0, of which waited for: 1 -> 0; matrix products, arithmetic and copies ran while one was open for 8% -> 0% of each run, Pallas kernels for 0% -> 0%
where the time goes in v2:
time: 143 us
  Pallas kernels  109 us (76%)
  matrix products  18.2 us (13%)
  local copies, waits for them, and re-layouts  10.7 us (7%)
  other arithmetic  4.99 us (3%)
    pallas_call x1, Pallas kernels, gathered(): pl.pallas_call(functools.partial(gather_kernel, devices[0] // 2), out_sha...  67 us
    pallas_call x1, Pallas kernels, mixer(): pl.pallas_call(functools.partial(mixer_kernel, spans, peers), out_shape=j...  41.6 us
    dot_general x1, matrix products, body(): lax.dot_general(hidden[0], gathered(input_weight), NT, preferred_element_...  18.2 us
    unnamed x9, local copies, waits for them, and re-layouts  4.31 us

profile of v2, /device:TPU:5, one launch (start us, length us, event | category | flops | bytes accessed | tf_op | source)
XLA Modules:
  0.0 142.5 jit_solution(12850234049293538732)
XLA Ops:
  0.0 67.0 %gather.1 = bf16[32,88,2560]{2,1,0:T(8,128)(2,1)} custom-call(bf16[88,2560]{1,0:T(8,128)(2,1)} %shard.1), custom_call_target="tpu_custom_call" | custom-call | tf_op jit(solution)/shard_map/gather/pallas_call | solution.py:473
  67.0 18.2 %convolution_convert_fusion.proj = bf16[768,2816]{1,0:T(8,128)(2,1)} fusion(bf16[2816,2560]{1,0:T(8,128)(2,1)} %bitcast.32, bf16[1,768,2560]{2,1,0:T(8,128)(2,1)} %param.6), kind=kOutput, calls=%fused_computation | convolution fusion | flops 11075125248 | bytes 22675456 | tf_op jit(solution)/shard_map/dot_general | solution.py:491
  85.2 0.7 pad_convert_fusion.taps
  85.9 0.6 broadcast_in_dim.17.bias
  86.5 1.8 %reduce-window.6 = f32[40,3,2,128]{3,0,1,2:T(8,128)S(1)} reduce-window(f32[40,3,2,128]{3,0,1,2:T(8,128)S(1)} %copy.31, f32[]{:T(128)} %constant.33.clone.1), window={size=1x1x1x128 pad=0_0x0_0x0_0x127_0}, to_apply=%region_0.0 | reduce-window | flops 3901440 | bytes 245764 | tf_op jit(solution)/shard_map/reduce-window
  88.3 0.1 slice.12
  88.4 0.1 copy.32
  88.6 0.1 broadcast_multiply_fusion
  88.7 0.2 copy.35
  88.9 0.2 copy.36
  89.1 0.2 slice_reduce_fusion
  89.3 0.1 bitcast_exponential_fusion
  89.4 0.3 maximum_bitcast_fusion
  89.7 0.8 pad.19.weight
  90.5 0.8 pad.20.growth
  91.3 1.1 and_convert_fusion.spread
  92.5 0.1 reshape.99
  92.6 0.6 pad.21.decay
  93.3 0.7 broadcast_in_dim_reshape.3.skip
  94.0 0.1 mul.12
  94.1 1.8 %copy.38.column = f32[5,768,8]{2,1,0:T(8,128)} copy(f32[5,768,8]{1,2,0:T(8,128)S(1)} %bitcast.34) | data formatting | bytes 245760 | tf_op jit(solution)/shard_map/transpose | solution.py:247
  96.0 0.7 bitcast_subtract_fusion.1.row
  96.7 41.6 %mixer.1 = bf16[768,2560]{1,0:T(8,128)(2,1)} custom-call(bf16[768,2816]{1,0:T(8,128)(2,1)} %convolution_convert_fusion.proj, f32[8,2816]{1,0:T(8,128)} %pad_convert_fusion.taps, f32[1,2816]{1,0:T(1,128)} %broadcast_in_dim.17.bias, f32[768,128]{1,0:T(8,128)} %pad.19.weight, f32[768,128]{1,0:T(8,128)} %pad.20.growth, ...), custom_call_target="tpu_custom_call" | custom-call | flops 8000000000 | bytes 16000000 | tf_op jit(solution)/shard_map/mixer/pallas_call | solution.py:258
  138.2 4.3 %copy.42 = bf16[1,768,2560]{2,1,0:T(8,128)(2,1)} copy(bf16[1,768,2560]{2,1,0:T(8,128)(2,1)} %bitcast.33) | data formatting | bytes 7864320
  (22 shorter events, 0.4 us)
Async XLA Ops:
  67.0 18.2 %copy-start.1 = (bf16[4,2816]{1,0:T(4,128)(2,1)S(1)}, bf16[4,2816]{1,0:T(4,128)(2,1)}, u32[]{:S(2)}) copy-start(bf16[4,2816]{1,0:T(4,128)(2,1)} %param.9) | copy-start | bytes 67588
  67.0 18.9 %copy-start.2 = (f32[2816]{0:T(1024)S(1)}, f32[2816]{0:T(1024)}, u32[]{:S(2)}) copy-start(f32[2816]{0:T(1024)} %param.10) | copy-start | bytes 33796
  67.0 19.5 %copy-start = (f32[1,40,768]{2,1,0:T(8,128)S(1)}, f32[1,40,768]{2,1,0:T(8,128)}, u32[]{:S(2)}) copy-start(f32[1,40,768]{2,1,0:T(8,128)} %param.7) | copy-start | bytes 368644
  88.4 4.8 %copy-start.3 = (f32[40]{0:T(128)S(1)}, f32[40]{0:T(128)}, u32[]{:S(2)}) copy-start(f32[40]{0:T(128)} %param.11) | copy-start | bytes 484

commit v3 on v2

--- a/solution.py
+++ b/solution.py
@@ -230,10 +230,9 @@
         state_copy.wait_send()
 
 
-def mixer(projected, log_decay, conv_weight, conv_bias, skip_gain):
-    length = projected.shape[0]
+def prepared(log_decay):
+    length = log_decay.shape[1]
     spans = length // SPAN
-    peers = lax.axis_size("seq")
     step = -log_decay
     cum = jnp.cumsum(log_decay.reshape(HEADS, spans, SPAN), axis=2)
     last = cum[:, :, -1:]
@@ -253,6 +252,14 @@
     head_of = jnp.arange(INNER)[None, :] // HEAD_DIM
     part = jnp.arange(128)[:, None]
     spread = ((part % HEADS == head_of) & (part < 2 * HEADS)).astype(BF16)
+    return doubled(weight), doubled(jnp.exp(flat)), spread, decay, column, row
+
+
+def mixer(projected, factors, conv_weight, conv_bias, skip_gain):
+    length = projected.shape[0]
+    spans = length // SPAN
+    peers = lax.axis_size("seq")
+    weight, growth, spread, decay, column, row = factors
     taps = jnp.pad(conv_weight.astype(F32), ((0, 8 - CONV), (0, 0)))
     vmem = pl.BlockSpec(memory_space=pltpu.VMEM)
     return pl.pallas_call(
@@ -282,8 +289,8 @@
         ),
         name="mixer",
     )(
-        projected, taps, conv_bias[None, :], doubled(weight), doubled(jnp.exp(flat)),
-        spread, decay, jnp.repeat(skip_gain, HEAD_DIM)[None, :], column, row,
+        projected, taps, conv_bias[None, :], weight, growth, spread, decay,
+        jnp.repeat(skip_gain, HEAD_DIM)[None, :], column, row,
     )
 
 
@@ -291,7 +298,53 @@
 BY_Z, BY_X, BY_Y, BY_X_HALF, BY_Y_HALF, FROM_OWN, FROM_X, FROM_Y, FROM_XY = range(9)
 
 
-def gather_kernel(layers, shard, whole, send_sems, up_sems, recv_sems, own_sem):
+def prepare(log_decay, weight, growth, spread, decay, column, row):
+    spans = log_decay.shape[1] // SPAN
+    width = 2 * HEAD_DIM * 2
+    for start in range(0, INNER, width):
+        part = lax.broadcasted_iota(jnp.int32, (128, width), 0)
+        head = jnp.where(part < HEADS, part, part - HEADS)
+        gap = start + lax.broadcasted_iota(jnp.int32, (128, width), 1) - head * HEAD_DIM
+        hit = (part < 2 * HEADS) & (gap >= 0) & (gap < HEAD_DIM)
+        spread[:, start : start + width] = jnp.where(hit, 1.0, 0.0).astype(BF16)
+    sooner = lax.broadcasted_iota(jnp.int32, (SPAN, SPAN), 0)
+    later = lax.broadcasted_iota(jnp.int32, (SPAN, SPAN), 1)
+    causal = jnp.where(sooner <= later, 1.0, 0.0)
+    pad = jnp.zeros((128 - 2 * HEADS, SPAN), F32)
+    more = jnp.zeros((128 - HEADS, SPAN), F32)
+    decay[...] = jnp.ones_like(decay)
+    for span in range(spans):
+        rows = slice(span * SPAN, (span + 1) * SPAN)
+        change = log_decay[:, rows]
+        step = -change
+        cum = jnp.dot(
+            change, causal, precision=lax.Precision.HIGHEST, preferred_element_type=F32
+        )
+        left = jnp.exp(cum[:, SPAN - 1 :] - cum) * step
+        grown = jnp.exp(cum)
+        weight[rows, :] = jnp.concatenate([left, left, pad], axis=0).T
+        growing = jnp.concatenate([grown, grown, pad], axis=0).T
+        growth[rows, :] = growing
+        scaled = cum * LOG2E
+        turned = jnp.concatenate([scaled, more], axis=0).T
+        shifted = scaled - jnp.log2(step)
+        for group in range(GROUPS):
+            heads = slice(group * GROUP, (group + 1) * GROUP)
+            column[group, rows, :] = turned[:, heads]
+            row[group, :, rows] = shifted[heads]
+        ends = split_parts(growing[SPAN - 8 :, :])
+        for start in range(0, INNER, width):
+            lanes = slice(start, start + width)
+            end = jnp.dot(ends, spread[:, lanes], preferred_element_type=F32)[7:8]
+            decay[span : span + 1, lanes] = end
+            decay[spans : spans + 1, lanes] = decay[spans : spans + 1, lanes] * end
+
+
+def gather_kernel(
+    layers, shard, log_decay,
+    whole, weight, growth, spread, decay, column, row,
+    send_sems, up_sems, recv_sems, own_sem,
+):
     dp, seq = lax.axis_index("dp"), lax.axis_index("seq")
     z, x = dp // 2, lax.rem(dp, 2)
     y, core = seq // 2, lax.rem(seq, 2)
@@ -433,6 +486,7 @@
         column_step(place)
         if place == 0:
             own.start()
+            prepare(log_decay, weight, growth, spread, decay, column, row)
         if place >= 2:
             plane_step(place - 2)
         if place >= 4:
@@ -464,37 +518,48 @@
                 copy(dst, dst, own_sem, recv_sems.at[place, kind], core_peer).wait_recv()
 
 
-def gathered(input_weight):
+def gathered(input_weight, log_decay):
     devices = lax.axis_size("dp"), lax.axis_size("seq")
-    if devices != (8, 4):
-        return lax.all_gather(input_weight, ("dp", "seq"), axis=0, tiled=True)
     rows, depth = input_weight.shape
+    length = log_decay.shape[1]
+    if devices != (8, 4) or length // SPAN > 7:
+        whole = lax.all_gather(input_weight, ("dp", "seq"), axis=0, tiled=True)
+        return whole, prepared(log_decay)
     anywhere = pl.BlockSpec(memory_space=pl.ANY)
-    whole = pl.pallas_call(
+    vmem = pl.BlockSpec(memory_space=pltpu.VMEM)
+    whole, *factors = pl.pallas_call(
         functools.partial(gather_kernel, devices[0] // 2),
-        out_shape=jax.ShapeDtypeStruct((devices[0] * devices[1], rows, depth), BF16),
-        in_specs=[anywhere],
-        out_specs=anywhere,
+        out_shape=[
+            jax.ShapeDtypeStruct((devices[0] * devices[1], rows, depth), BF16),
+            jax.ShapeDtypeStruct((length, 128), F32),
+            jax.ShapeDtypeStruct((length, 128), F32),
+            jax.ShapeDtypeStruct((128, INNER), BF16),
+            jax.ShapeDtypeStruct((8, INNER), F32),
+            jax.ShapeDtypeStruct((GROUPS, length, GROUP), F32),
+            jax.ShapeDtypeStruct((GROUPS, GROUP, length), F32),
+        ],
+        in_specs=[anywhere, vmem],
+        out_specs=[anywhere] + [vmem] * 6,
         scratch_shapes=[
             pltpu.SemaphoreType.DMA((7, 9)),
             pltpu.SemaphoreType.DMA((7,)),
             pltpu.SemaphoreType.DMA((7, 9)),
             pltpu.SemaphoreType.DMA,
         ],
-        compiler_params=pltpu.CompilerParams(collective_id=1, has_side_effects=True),
+        compiler_params=pltpu.CompilerParams(
+            collective_id=1, has_side_effects=True, vmem_limit_bytes=20 * 2**20
+        ),
         name="gather",
-    )(input_weight)
-    return whole.reshape(devices[0] * devices[1] * rows, depth)
+    )(input_weight, log_decay)
+    return whole.reshape(devices[0] * devices[1] * rows, depth), factors
 
 
 def body(hidden, log_decay, input_weight, conv_weight, conv_bias, skip_gain):
+    whole, factors = gathered(input_weight, log_decay[0])
     projected = lax.dot_general(
-        hidden[0],
-        gathered(input_weight),
-        NT,
-        preferred_element_type=F32,
+        hidden[0], whole, NT, preferred_element_type=F32
     ).astype(BF16)
-    return mixer(projected, log_decay[0], conv_weight, conv_bias, skip_gain)[None]
+    return mixer(projected, factors, conv_weight, conv_bias, skip_gain)[None]
 
 
 def solution(mesh):

time: 143 us -> 135 us (0.944)
  other arithmetic: 4.99 us -> 0.64 us
  matrix products: 18.2 us -> 14.2 us
  local copies, waits for them, and re-layouts: 10.7 us -> 12.5 us
    unnamed x9 -> x23, local copies, waits for them, and re-layouts: 4.31 us -> 11.1 us
    dot_general x1, matrix products: 18.2 us -> 14.2 us  [body(): lax.dot_general(hidden[0], whole, NT, preferred_element_type=F32)]
    pad x3 -> x0, local copies, waits for them, and re-layouts: 2.2 us -> none  [the longest x2 1.56 us: doubled(): jnp.pad(jnp.concatenate([a, a], axis=0).T, ((0, 0), (0, 128 - 2 * HEADS)))]
    transpose x1 -> x0, local copies, waits for them, and re-layouts: 1.85 us -> none  [mixer(): column = grouped.transpose(0, 2, 1)]
    another operation x2 -> x0, other arithmetic: 1.81 us -> none
where the time goes in v3:
time: 135 us
  Pallas kernels  108 us (80%)
  matrix products  14.2 us (11%)
  local copies, waits for them, and re-layouts  12.5 us (9%)
    pallas_call x1, Pallas kernels, gathered(): pl.pallas_call(functools.partial(gather_kernel, devices[0] // 2), out_sha...  66 us
    pallas_call x1, Pallas kernels, mixer(): pl.pallas_call(functools.partial(mixer_kernel, spans, peers), out_shape=j...  41.6 us
    dot_general x1, matrix products, body(): lax.dot_general(hidden[0], whole, NT, preferred_element_type=F32)  14.2 us
    unnamed x23, local copies, waits for them, and re-layouts  11.1 us

profile of v3, /device:TPU:5, one launch (start us, length us, event | category | flops | bytes accessed | tf_op | source)
XLA Modules:
  0.0 135.0 jit_solution(2230016085127922667)
XLA Ops:
  0.0 0.0 copy-start
  0.0 1.0 copy-done
  1.0 0.0 copy-start.1
  1.0 0.9 copy-done.1
  1.9 66.0 %gather.1 = (bf16[32,88,2560]{2,1,0:T(8,128)(2,1)S(1)}, f32[768,128]{1,0:T(8,128)S(1)}, f32[768,128]{1,0:T(8,128)S(1)}, bf16[128,2560]{1,0:T(8,128)(2,1)S(1)}, f...) custom-call(bf16[88,2560]{1,0:T(8,128)(2,1)S(1)} %copy-done, f32[40,768]{1,0:T(8,128)S(1)} %bitcast.9), custom_call_target="tpu_custom_call" | custom-call | tf_op jit(solution)/shard_map/gather/pallas_call | solution.py:530
  67.9 0.0 copy-start.2
  67.9 1.3 copy-done.2
  69.2 0.0 copy-start.3
  69.2 0.9 copy-done.3
  70.0 0.0 copy-start.4
  70.1 0.8 copy-done.4
  70.8 0.7 copy-done.5
  71.6 0.6 copy-done.6
  72.2 0.6 copy-done.7
  72.8 14.2 %fusion.proj = bf16[768,2816]{1,0:T(8,128)(2,1)} fusion(bf16[2816,2560]{1,0:T(8,128)(2,1)S(1)} %bitcast.10, bf16[1,768,2560]{2,1,0:T(8,128)(2,1)} %param.6), kind=kOutput, calls=%fused_computation.1 | convolution fusion | flops 11075125248 | bytes 22675456 | tf_op jit(solution)/shard_map/dot_general | solution.py:559
  87.1 0.0 copy-done.8
  87.1 0.6 pad_convert_fusion.taps
  87.7 0.0 copy-done.10
  87.7 0.1 broadcast_in_dim.10
  87.8 0.7 broadcast_in_dim_reshape.3.skip
  88.5 0.0 copy-done.9
  88.5 0.6 broadcast_in_dim.9.bias
  89.1 41.6 %mixer.1 = bf16[768,2560]{1,0:T(8,128)(2,1)} custom-call(bf16[768,2816]{1,0:T(8,128)(2,1)} %fusion.proj, f32[8,2816]{1,0:T(8,128)} %pad_convert_fusion.taps, f32[1,2816]{1,0:T(1,128)} %broadcast_in_dim.9.bias, f32[768,128]{1,0:T(8,128)} %copy-done.4, f32[768,128]{1,0:T(8,128)} %copy-done.5, bf16[128,2560]{1,0:T(8,128)(2,1)} %copy-done.3, ...), custom_call_target="tpu_custom_call" | custom-call | flops 8000000000 | bytes 16000000 | tf_op jit(solution)/shard_map/mixer/pallas_call | solution.py:265
  130.7 4.3 %copy.10 = bf16[1,768,2560]{2,1,0:T(8,128)(2,1)} copy(bf16[1,768,2560]{2,1,0:T(8,128)(2,1)} %bitcast.11) | data formatting | bytes 7864320
  (6 shorter events, 0.0 us)
Async XLA Ops:
  0.0 1.0 copy-start
  1.0 0.9 copy-start.1
  67.9 1.3 copy-start.2
  69.2 0.9 copy-start.3
  70.0 0.8 copy-start.4
  70.8 0.7 copy-start.5
  71.6 0.6 copy-start.6
  72.2 0.6 copy-start.7
  72.8 14.3 %copy-start.8 = (bf16[4,2816]{1,0:T(4,128)(2,1)S(1)}, bf16[4,2816]{1,0:T(4,128)(2,1)}, u32[]{:S(2)}) copy-start(bf16[4,2816]{1,0:T(4,128)(2,1)} %param.9) | copy-start | bytes 67588
  72.8 14.9 %copy-start.10 = (f32[40]{0:T(128)S(1)}, f32[40]{0:T(128)}, u32[]{:S(2)}) copy-start(f32[40]{0:T(128)} %param.11) | copy-start | bytes 484
  72.8 15.7 %copy-start.9 = (f32[2816]{0:T(1024)S(1)}, f32[2816]{0:T(1024)}, u32[]{:S(2)}) copy-start(f32[2816]{0:T(1024)} %param.10) | copy-start | bytes 33796

commit v4 on v3

--- a/solution.py
+++ b/solution.py
@@ -35,7 +35,7 @@
     spans, peers,
     proj, taps, bias, weight, growth, spread, decay, skip, column, row,
     out,
-    halo, previous, act, bt, states, local, total, scores, sending, entering,
+    halo, previous, act, bt, states, local, total, scores, sending, entering, growing,
     halo_sems, state_sems,
 ):
     place = lax.axis_index("seq")
@@ -110,10 +110,12 @@
                 for k in range(CONV - 1):
                     at = 8 - (CONV - 1) + k
                     value = value + both[at : at + TILE] * tap[k]
-                act[pl.ds(start, TILE), lanes] = (value / (1.0 + jnp.exp(-value))).astype(BF16)
+                halved = 0.5 * value
+                act[pl.ds(start, TILE), lanes] = (halved + halved * jnp.tanh(halved)).astype(BF16)
 
         bt[...] = act[rows, INNER : INNER + STATE].astype(F32).T.astype(BF16)
         parts = split_parts(weight[rows, :])
+        growing[rows, :] = split_parts(growth[rows, :])
 
         @pl.loop(0, INNER // CHUNK)
         def _(chunk):
@@ -214,9 +216,7 @@
         held = entering[:, lanes].astype(F32)
         for span in range(spans):
             rows = pl.ds(span * SPAN, SPAN)
-            grown = jnp.dot(
-                split_parts(growth[rows, :]), spread[:, lanes], preferred_element_type=F32
-            )
+            grown = jnp.dot(growing[rows, :], spread[:, lanes], preferred_element_type=F32)
             read = jnp.dot(
                 act[rows, INNER + STATE :], held.astype(BF16), preferred_element_type=F32
             )
@@ -278,6 +278,7 @@
             pltpu.VMEM((SPAN, SPAN), F32),
             pltpu.VMEM((STATE, INNER), BF16),
             pltpu.VMEM((STATE, INNER), BF16),
+            pltpu.VMEM((length, 128), BF16),
             pltpu.SemaphoreType.DMA((2,)),
             pltpu.SemaphoreType.DMA((2,)),
         ],

time: 135 us -> 135 us (level)
  no operation moved by 1% of the time
where the time goes in v4:
time: 135 us; the launch traced here: 134 us
  Pallas kernels  107 us (79%)
  matrix products  14.2 us (11%)
  local copies, waits for them, and re-layouts  12.5 us (9%)
    pallas_call x1, Pallas kernels, gathered(): pl.pallas_call(functools.partial(gather_kernel, devices[0] // 2), out_sha...  66 us
    pallas_call x1, Pallas kernels, mixer(): pl.pallas_call(functools.partial(mixer_kernel, spans, peers), out_shape=j...  40.9 us
    dot_general x1, matrix products, body(): lax.dot_general(hidden[0], whole, NT, preferred_element_type=F32)  14.2 us
    unnamed x23, local copies, waits for them, and re-layouts  11.1 us

profile of v4, /device:TPU:5, one launch (start us, length us, event | category | flops | bytes accessed | tf_op | source)
XLA Modules:
  0.0 134.3 jit_solution(4468129119641502485)
XLA Ops:
  0.0 0.0 copy-start
  0.0 1.0 copy-done
  1.0 0.0 copy-start.1
  1.0 0.9 copy-done.1
  1.9 66.0 %gather.1 = (bf16[32,88,2560]{2,1,0:T(8,128)(2,1)S(1)}, f32[768,128]{1,0:T(8,128)S(1)}, f32[768,128]{1,0:T(8,128)S(1)}, bf16[128,2560]{1,0:T(8,128)(2,1)S(1)}, f...) custom-call(bf16[88,2560]{1,0:T(8,128)(2,1)S(1)} %copy-done, f32[40,768]{1,0:T(8,128)S(1)} %bitcast.9), custom_call_target="tpu_custom_call" | custom-call | tf_op jit(solution)/shard_map/gather/pallas_call | solution.py:531
  67.9 0.0 copy-start.2
  67.9 1.3 copy-done.2
  69.2 0.0 copy-start.3
  69.2 0.9 copy-done.3
  70.0 0.0 copy-start.4
  70.1 0.8 copy-done.4
  70.8 0.7 copy-done.5
  71.6 0.6 copy-done.6
  72.2 0.6 copy-done.7
  72.8 14.2 %fusion.proj = bf16[768,2816]{1,0:T(8,128)(2,1)} fusion(bf16[2816,2560]{1,0:T(8,128)(2,1)S(1)} %bitcast.10, bf16[1,768,2560]{2,1,0:T(8,128)(2,1)} %param.6), kind=kOutput, calls=%fused_computation.1 | convolution fusion | flops 11075125248 | bytes 22675456 | tf_op jit(solution)/shard_map/dot_general | solution.py:560
  87.1 0.0 copy-done.8
  87.1 0.6 pad_convert_fusion.taps
  87.7 0.0 copy-done.10
  87.7 0.1 broadcast_in_dim.10
  87.8 0.7 broadcast_in_dim_reshape.3.skip
  88.5 0.0 copy-done.9
  88.5 0.6 broadcast_in_dim.9.bias
  89.1 40.9 %mixer.1 = bf16[768,2560]{1,0:T(8,128)(2,1)} custom-call(bf16[768,2816]{1,0:T(8,128)(2,1)} %fusion.proj, f32[8,2816]{1,0:T(8,128)} %pad_convert_fusion.taps, f32[1,2816]{1,0:T(1,128)} %broadcast_in_dim.9.bias, f32[768,128]{1,0:T(8,128)} %copy-done.4, f32[768,128]{1,0:T(8,128)} %copy-done.5, bf16[128,2560]{1,0:T(8,128)(2,1)} %copy-done.3, ...), custom_call_target="tpu_custom_call" | custom-call | flops 8000000000 | bytes 16000000 | tf_op jit(solution)/shard_map/mixer/pallas_call | solution.py:265
  130.0 4.3 %copy.10 = bf16[1,768,2560]{2,1,0:T(8,128)(2,1)} copy(bf16[1,768,2560]{2,1,0:T(8,128)(2,1)} %bitcast.11) | data formatting | bytes 7864320
  (6 shorter events, 0.0 us)
Async XLA Ops:
  0.0 1.0 copy-start
  1.0 0.9 copy-start.1
  67.9 1.3 copy-start.2
  69.2 0.9 copy-start.3
  70.0 0.8 copy-start.4
  70.8 0.7 copy-start.5
  71.6 0.6 copy-start.6
  72.2 0.6 copy-start.7
  72.8 14.3 %copy-start.8 = (bf16[4,2816]{1,0:T(4,128)(2,1)S(1)}, bf16[4,2816]{1,0:T(4,128)(2,1)}, u32[]{:S(2)}) copy-start(bf16[4,2816]{1,0:T(4,128)(2,1)} %param.9) | copy-start | bytes 67588
  72.8 14.9 %copy-start.10 = (f32[40]{0:T(128)S(1)}, f32[40]{0:T(128)}, u32[]{:S(2)}) copy-start(f32[40]{0:T(128)} %param.11) | copy-start | bytes 484
  72.8 15.7 %copy-start.9 = (f32[2816]{0:T(1024)S(1)}, f32[2816]{0:T(1024)}, u32[]{:S(2)}) copy-start(f32[2816]{0:T(1024)} %param.10) | copy-start | bytes 33796
